TPU v7x, 32 devices: a whole 2x2x4 slice. The times are simulated.
32 devices in a mesh: chan: 4 (over y, core), tile: 8 (over z, x).
Axes of the slice: x: 2, y: 2, z: 4, core: 2. Of those that a mesh axis runs over, the one named last changes fastest.
Arguments:
- intensity: bfloat16 [256, 256, 512], P('chan', 'tile'), may hold values from -12 to 12
- block_pick: int32 [8, 4, 4], P('tile', 'chan'), may hold values from 0 to 7, as said below
- owner_tile: int32 [8, 4, 4], P('tile', 'chan'), may hold values from 0 to 7, as said below
- source_index: int32 [8, 4, 4], P('tile', 'chan'), may hold values from 0 to 15
- mask_low: int32 [8, 4, 4, 1024], P('tile', 'chan'), may hold values from 0 to 63
- mask_high: int32 [8, 4, 4, 1024], P('tile', 'chan'), may hold values from 64 to 128
Outputs:
- moment_maps: float32 [8, 4, 8, 2, 1024], P('tile', 'chan')
- spectra: float32 [8, 4, 16, 256], P('tile', 'chan')
- smoothed: bfloat16 [256, 256, 512], P(None, 'tile', 'chan')
Inputs may be any that keep to these rules, and one draw needn't show every extreme that they name: `block_pick`: the 4 block numbers of one device are distinct. `owner_tile`: among the 4 sends of one device no owner appears more than 2 times; in every chan index some owner receives exactly 2 blocks from every device of that chan index.
All inputs are finite; a program needn't handle non-finite values.
Results may differ from a plain program's by a relative error of at most 0.0021.
Values may be sent and summed in bfloat16 or wider, within the bound.
A program may use at most 128 MiB of HBM per device.

v0:
```python
import jax
import jax.numpy as jnp
from jax import lax
from jax.sharding import PartitionSpec as P

BCH = 128
BPIX = 32
RADIUS = 2
CAP = 2
SRC_DEV = 16
SIGMA = 1.5


def with_halo(block, sides, width):
    for axis, dim in sides:
        count = lax.axis_size(axis)
        forward = [(i, i + 1) for i in range(count - 1)]
        backward = [(target, source) for source, target in forward]
        low = lax.ppermute(
            lax.slice_in_dim(block, block.shape[dim] - width, None, axis=dim), axis, forward
        )
        high = lax.ppermute(lax.slice_in_dim(block, 0, width, axis=dim), axis, backward)
        block = jnp.concatenate([low, block, high], axis=dim)
    return block


def gauss_weights():
    offsets = jnp.arange(-RADIUS, RADIUS + 1).astype(jnp.float32)
    raw_weights = jnp.exp(-offsets * offsets / (2.0 * SIGMA * SIGMA))
    return raw_weights / jnp.sum(raw_weights)


def smooth_tiles(framed):
    chan_total = framed.shape[0]
    rows_inner = framed.shape[1] - 2 * RADIUS
    cols_inner = framed.shape[2] - 2 * RADIUS
    chan_blocks = chan_total // BCH
    weights = gauss_weights()

    def smooth_block(block_index):
        first_chan = block_index * BCH
        middle = lax.dynamic_slice_in_dim(framed, first_chan, BCH, 0).astype(jnp.float32)
        before = lax.dynamic_slice_in_dim(framed, jnp.maximum(first_chan - 1, 0), 1, 0).astype(
            jnp.float32
        )
        before = before * (block_index > 0).astype(jnp.float32)
        after = lax.dynamic_slice_in_dim(
            framed, jnp.minimum(first_chan + BCH, chan_total - 1), 1, 0
        ).astype(jnp.float32)
        after = after * (block_index < chan_blocks - 1).astype(jnp.float32)
        lower = jnp.concatenate([before, middle[:-1]], axis=0)
        upper = jnp.concatenate([middle[1:], after], axis=0)
        hanning = 0.5 * middle + 0.25 * (lower + upper)
        row_pass = sum(
            (
                weights[offset] * hanning[:, offset : offset + rows_inner, :]
                for offset in range(2 * RADIUS + 1)
            )
        )
        col_pass = sum(
            (
                weights[offset] * row_pass[:, :, offset : offset + cols_inner]
                for offset in range(2 * RADIUS + 1)
            )
        )
        return col_pass.astype(jnp.bfloat16)

    stacked = lax.map(smooth_block, jnp.arange(chan_blocks, dtype=jnp.int32))
    return stacked.reshape(chan_total, rows_inner, cols_inner)


def per_device(intensity, block_pick, owner_tile, source_index, mask_low, mask_high):
    regrouped = lax.all_to_all(intensity, "chan", split_axis=2, concat_axis=0, tiled=True)
    framed = with_halo(regrouped, (("chan", 2), ("tile", 1)), RADIUS)
    tile_cube = smooth_tiles(framed)
    chan_total, rows_inner, cols_inner = tile_cube.shape
    chan_blocks = chan_total // BCH
    block_rows = rows_inner // BPIX
    block_cols = cols_inner // BPIX
    per_chan_block = block_rows * block_cols
    pixel_count = mask_low.shape[-1]
    picks = block_pick.reshape(-1)
    owners = owner_tile.reshape(-1)
    sources = source_index.reshape(-1)
    send_count = picks.shape[0]
    low_rows = mask_low.reshape(send_count, pixel_count)
    high_rows = mask_high.reshape(send_count, pixel_count)
    chan_of = picks // per_chan_block
    positions = jnp.arange(send_count, dtype=jnp.int32)
    earlier = (positions[None, :] < positions[:, None]) & (owners[None, :] == owners[:, None])
    ranking = jnp.sum(earlier.astype(jnp.int32), axis=1)
    slot_of = owners * CAP + ranking
    peer_count = lax.axis_size("tile")
    slot_total = peer_count * CAP
    filled = slot_of[None, :] == jnp.arange(slot_total, dtype=jnp.int32)[:, None]
    occupied = jnp.any(filled, axis=1)
    sender = jnp.sum(jnp.where(filled, positions[None, :], 0), axis=1)
    tags = jnp.stack([jnp.where(occupied, sources[sender], -1), chan_of[sender]], axis=1).reshape(
        peer_count, CAP, 2
    )
    block_total = chan_blocks * per_chan_block
    low_grid = jnp.zeros((block_total, pixel_count), jnp.int32).at[picks].set(low_rows)
    high_grid = jnp.zeros((block_total, pixel_count), jnp.int32).at[picks].set(high_rows)

    def to_tile(grid):
        shaped = grid.reshape(chan_blocks, block_rows, block_cols, BPIX, BPIX).transpose(
            0, 1, 3, 2, 4
        )
        return shaped.reshape(chan_blocks, 1, rows_inner, cols_inner)

    low_tile = to_tile(low_grid)
    high_tile = to_tile(high_grid)
    cube_blocks = tile_cube.reshape(chan_blocks, BCH, rows_inner, cols_inner)
    chan_pos = jnp.arange(BCH, dtype=jnp.int32).reshape(1, BCH, 1, 1)
    inside = (low_tile <= chan_pos) & (chan_pos < high_tile)
    masked = jnp.where(inside, cube_blocks.astype(jnp.float32), 0.0)
    maps_tile = jnp.sum(masked, axis=1)
    spectra_tile = jnp.sum(
        masked.reshape(chan_blocks, BCH, block_rows, BPIX, block_cols, BPIX), axis=(3, 5)
    )
    all_maps = (
        maps_tile.reshape(chan_blocks, block_rows, BPIX, block_cols, BPIX)
        .transpose(0, 1, 3, 2, 4)
        .reshape(block_total, pixel_count)
    )
    all_spectra = spectra_tile.transpose(0, 2, 3, 1).reshape(block_total, BCH)
    slot_picks = picks[sender]
    maps_slots = jnp.where(occupied[:, None], all_maps[slot_picks], 0.0).reshape(
        peer_count, CAP, pixel_count
    )
    spectra_slots = jnp.where(occupied[:, None], all_spectra[slot_picks], 0.0).reshape(
        peer_count, CAP, BCH
    )
    maps_here, spectra_here, tags_here = (
        lax.all_to_all(maps_slots, "tile", split_axis=0, concat_axis=0, tiled=True),
        lax.all_to_all(spectra_slots, "tile", split_axis=0, concat_axis=0, tiled=True),
        lax.all_to_all(tags, "tile", split_axis=0, concat_axis=0, tiled=True),
    )
    moment_maps = maps_here.reshape(1, 1, peer_count, CAP, pixel_count)
    keys_here = (tags_here[..., 0] * chan_blocks + tags_here[..., 1]).reshape(-1)
    selector = (
        keys_here[None, :] == jnp.arange(SRC_DEV * chan_blocks, dtype=jnp.int32)[:, None]
    ).astype(jnp.float32)
    spectra = jnp.dot(
        selector,
        spectra_here.reshape(-1, BCH),
        precision=lax.Precision.HIGHEST,
        preferred_element_type=jnp.float32,
    )
    return (moment_maps, spectra.reshape(1, 1, SRC_DEV, chan_blocks * BCH), tile_cube)


def solution(mesh):
    return jax.shard_map(
        per_device,
        mesh=mesh,
        in_specs=(
            P("chan", "tile", None),
            P("tile", "chan", None),
            P("tile", "chan", None),
            P("tile", "chan", None),
            P("tile", "chan", None, None),
            P("tile", "chan", None, None),
        ),
        out_specs=(
            P("tile", "chan", None, None, None),
            P("tile", "chan", None, None),
            P(None, "tile", "chan"),
        ),
        check_vma=False,
    )
```

profile of v0, /device:TPU:4, one launch (start us, length us, event | category | flops | bytes accessed | tf_op | source)
XLA Modules:
  0.0 183.7 jit_solution(6895373197032733767)
XLA Ops:
  0.6 8.8 %copy.87 = bf16[64,32,512]{0,1,2:T(8,128)(2,1)} copy(bf16[64,32,512]{2,1,0:T(8,128)(2,1)} %param.8) | data formatting | bytes 4194304 | tf_op args[0]
  9.4 5.9 %reshape.268 = bf16[4,2,131072]{2,1,0:T(2,128)(2,1)} reshape(bf16[512,32,64]{2,1,0:T(8,128)(2,1)} %bitcast.84) | data formatting | bytes 4194304
  15.3 3.7 %all-to-all-start = ((bf16[4,2,131072]{2,1,0:T(2,128)(2,1)}), bf16[4,2,131072]{2,1,0:T(2,128)(2,1)S(1)}, u32[]{:S(2)}, u32[]{:S(2)}) async-start(bf16[4,2,131072]{2,1,0:T(2,128)(2,1)} %reshape.268), calls=%async_computation | async-start | bytes 4194304 | tf_op jit(solution)/shard_map/all_to_all | solution.py:73
  22.3 20.5 %all-to-all-done = bf16[4,2,131072]{2,1,0:T(2,128)(2,1)S(1)} async-done(((bf16[4,2,131072]{2,1,0:T(2,128)(2,1)}), bf16[4,2,131072]{2,1,0:T(2,128)(2,1)S(1)}, u32[]{:S(2)}, u32[]{:S(2)}) %all-to-all-start) | async-done | bytes 2097184 | tf_op jit(solution)/shard_map/all_to_all | solution.py:73
  42.8 6.6 %all-to-all-start.2 = ((s32[8,2,2]{1,2,0:T(2,128)}), s32[8,2,2]{1,2,0:T(2,128)S(1)}, u32[]{:S(2)}, u32[]{:S(2)}) async-start(s32[8,2,2]{1,2,0:T(2,128)} %copy.98), calls=%async_computation.2 | async-start | bytes 16384 | tf_op jit(solution)/shard_map/all_to_all | solution.py:137
  49.4 4.0 %reshape.269 = bf16[512,32,64]{2,1,0:T(8,128)(2,1)} reshape(bf16[4,2,131072]{2,1,0:T(2,128)(2,1)S(1)} %all-to-all-done) | data formatting | bytes 4194304
  53.4 6.8 %copy.102 = bf16[64,32,4,128]{3,2,1,0:T(4,128)(2,1)} copy(bf16[64,32,4,128]{0,1,3,2:T(8,128)(2,1)} %bitcast.83) | data formatting | bytes 4194304 | tf_op jit(solution)/shard_map/all_to_all | solution.py:73
  70.3 3.3 %copy.91 = bf16[256,32,2]{0,1,2:T(8,128)(2,1)S(1)} copy(bf16[256,32,2]{2,1,0:T(8,128)(2,1)} %get-tuple-element.93) | data formatting | bytes 65536 | tf_op jit(solution)/shard_map/slice | solution.py:22
  73.6 3.8 %collective-permute-start.1 = (bf16[256,32,2]{0,1,2:T(8,128)(2,1)S(1)}, bf16[256,32,2]{0,1,2:T(8,128)(2,1)S(1)}, u32[]{:S(2)}, u32[]{:S(2)}) collective-permute-start(bf16[256,32,2]{0,1,2:T(8,128)(2,1)S(1)} %copy.91), channel_id=1, source_target_pairs={{8,0},{16,8},{24,16},{9,1},{17,9},{25,17},{10,2},{18,10},{26,18},{... | collective-permute-start | bytes 98312 | tf_op jit(solution)/shard_map/ppermute | solution.py:22
  78.0 4.2 %copy.92 = bf16[256,32,2]{2,1,0:T(8,128)(2,1)} copy(bf16[256,32,2]{0,1,2:T(8,128)(2,1)S(1)} %collective-permute-done) | data formatting | bytes 65536 | tf_op jit(solution)/shard_map/ppermute | solution.py:19
  82.3 4.2 %copy.93 = bf16[256,32,2]{2,1,0:T(8,128)(2,1)} copy(bf16[256,32,2]{0,1,2:T(8,128)(2,1)S(1)} %collective-permute-done.1) | data formatting | bytes 65536 | tf_op jit(solution)/shard_map/ppermute | solution.py:22
  86.5 4.3 %pad_maximum_fusion = bf16[256,32,132]{2,1,0:T(8,128)(2,1)S(1)} fusion(bf16[256,32,2]{2,1,0:T(8,128)(2,1)} %copy.93, bf16[256,32,128]{2,1,0:T(8,128)(2,1)S(1)} %bitcast.82, bf16[256,32,2]{2,1,0:T(8,128)(2,1)} %copy.92), kind=kLoop, calls=%fused_computation.33 | loop fusion | flops 6488064 | bytes 4325376 | tf_op jit(solution)/shard_map/concatenate | solution.py:23
  93.1 3.9 %collective-permute-start.2 = (bf16[256,2,132]{2,1,0:T(2,128)(2,1)S(1)}, bf16[256,2,132]{2,1,0:T(2,128)(2,1)S(1)}, u32[]{:S(2)}, u32[]{:S(2)}) collective-permute-start(bf16[256,2,132]{2,1,0:T(2,128)(2,1)S(1)} %get-tuple-element.90), channel_id=1, source_target_pairs={{0,1},{1,2},{2,3},{3,4},{4,5},{5,6},{6,7},{8,9},{9,10},{10,11},{11... | collective-permute-start | bytes 405512 | tf_op jit(solution)/shard_map/ppermute | solution.py:19
  101.3 7.6 %copy.95 = bf16[256,32,132]{0,2,1:T(8,128)(2,1)} copy(bf16[256,32,132]{2,1,0:T(8,128)(2,1)} %copy-done.5) | data formatting | bytes 4325376 | tf_op jit(solution)/shard_map/concatenate | solution.py:23
  111.2 38.9 %while.12 = (s32[]{:T(128)}, bf16[2,128,32,128]{1,3,2,0:T(8,128)(2,1)}, f32[5]{0:T(128)S(1)}, s32[2]{0:T(128)S(1)}, bf16[256,36,132]{0,2,1:T(8,128)(2,1)S(1)}, /...) while((s32[]{:T(128)}, ...), condition=%wide.region_6.7_spmd, body=%wide.region_5.6_spmd.sunk | while | flops 14994001 | bytes 46544248 | solution.py:68
  121.4 3.8 %fusion.43 = f32[128,32,132]{0,2,1:T(8,128)S(1)} fusion(f32[128,36,132]{0,2,1:T(8,128)S(1)} %fusion.41, f32[]{:T(128)} %bitcast.74, f32[]{:T(128)} %bitcast.75, f32[]{:T(128)} %bitcast.76, f32[]{:T(128)} %bitcast.77, f32[]{:T(128)} %bitcast.78), kind=kLoop, calls=%fused_computation.13.clone.1 | loop fusion | flops 4866048 | bytes 12976148 | tf_op jit(solution)/shard_map/while/body/eval_jaxpr/add | solution.py:54
  125.3 5.4 %bitcast_dynamic-update-slice_fusion.2 = bf16[2,128,32,128]{1,3,2,0:T(8,128)(2,1)} fusion(bf16[2,128,32,128]{1,3,2,0:T(8,128)(2,1)} %get-tuple-element.158, s32[]{:T(128)} %get-tuple-element.157, f32[128,32,132]{0,2,1:T(8,128)S(1)} %fusion.43, f32[]{:T(128)} %bitcast.74, f32[]{:T(128)} %bitcast.75, f32[]{:T(128)} %bitcast.76, f32[]{:T(128)} %bitcast.77, ...), kind=kLoop, calls=%fused_computation.32.clone.1 | loop fusion | flops 5242880 | bytes 11537408 | tf_op jit(solution)/shard_map/while/body/jit(dynamic_update_index_in_dim)/dynamic_update_slice | solution.py:68
  140.9 3.8 %fusion.43 = f32[128,32,132]{0,2,1:T(8,128)S(1)} fusion(f32[128,36,132]{0,2,1:T(8,128)S(1)} %fusion.41, f32[]{:T(128)} %bitcast.74, f32[]{:T(128)} %bitcast.75, f32[]{:T(128)} %bitcast.76, f32[]{:T(128)} %bitcast.77, f32[]{:T(128)} %bitcast.78), kind=kLoop, calls=%fused_computation.13.clone.1 | loop fusion | flops 4866048 | bytes 12976148 | tf_op jit(solution)/shard_map/while/body/eval_jaxpr/add | solution.py:54
  144.7 5.4 %bitcast_dynamic-update-slice_fusion.2 = bf16[2,128,32,128]{1,3,2,0:T(8,128)(2,1)} fusion(bf16[2,128,32,128]{1,3,2,0:T(8,128)(2,1)} %get-tuple-element.158, s32[]{:T(128)} %get-tuple-element.157, f32[128,32,132]{0,2,1:T(8,128)S(1)} %fusion.43, f32[]{:T(128)} %bitcast.74, f32[]{:T(128)} %bitcast.75, f32[]{:T(128)} %bitcast.76, f32[]{:T(128)} %bitcast.77, ...), kind=kLoop, calls=%fused_computation.32.clone.1 | loop fusion | flops 5242880 | bytes 11537408 | tf_op jit(solution)/shard_map/while/body/jit(dynamic_update_index_in_dim)/dynamic_update_slice | solution.py:68
  150.1 6.1 %fusion.11 = (f32[2,128,128]{1,2,0:T(8,128)S(1)}, f32[2,32,128]{2,1,0:T(8,128)S(1)}) fusion(bf16[2,128,32,128]{1,3,2,0:T(8,128)(2,1)} %get-tuple-element.68, s32[2,32,128]{2,1,0:T(8,128)S(1)} %lt.89, s32[2,32,128]{2,1,0:T(8,128)S(1)} %le.17), kind=kLoop, calls=%fused_computation.35 | loop fusion | flops 7299072 | bytes 2326528 | tf_op jit(solution)/shard_map/reduce_sum | solution.py:118
  157.5 6.6 %all-to-all-start.3 = ((f32[8,2,128]{2,1,0:T(2,128)}), f32[8,2,128]{2,1,0:T(2,128)S(1)}, u32[]{:S(2)}, u32[]{:S(2)}) async-start(f32[8,2,128]{2,1,0:T(2,128)} %broadcast_select_fusion.1), calls=%async_computation.3 | async-start | bytes 16384 | tf_op jit(solution)/shard_map/all_to_all | solution.py:136
  165.7 4.5 %copy.101 = bf16[2,128,32,128]{3,2,1,0:T(8,128)(2,1)} copy(bf16[2,128,32,128]{1,3,2,0:T(8,128)(2,1)} %get-tuple-element.68) | data formatting | bytes 4194304 | tf_op jit(solution)/shard_map/while | solution.py:68
  170.6 5.6 %all-to-all-start.1 = ((f32[8,2,1024]{2,1,0:T(2,128)}), f32[8,2,1024]{2,1,0:T(2,128)S(1)}, u32[]{:S(2)}, u32[]{:S(2)}) async-start(f32[8,2,1024]{2,1,0:T(2,128)} %broadcast_select_fusion), calls=%async_computation.1 | async-start | bytes 131072 | tf_op jit(solution)/shard_map/all_to_all | solution.py:135
  176.9 6.2 %all-to-all-done.1 = f32[8,2,1024]{2,1,0:T(2,128)S(1)} async-done(((f32[8,2,1024]{2,1,0:T(2,128)}), f32[8,2,1024]{2,1,0:T(2,128)S(1)}, u32[]{:S(2)}, u32[]{:S(2)}) %all-to-all-start.1) | async-done | bytes 65568 | tf_op jit(solution)/shard_map/all_to_all | solution.py:135
  (92 shorter events, 43.8 us)
Async XLA Ops:
  0.6 98.4 %copy-start = (s32[1,1,4,1024]{3,2,1,0:T(4,128)S(1)}, s32[1,1,4,1024]{3,2,1,0:T(4,128)}, u32[]{:S(2)}) copy-start(s32[1,1,4,1024]{3,2,1,0:T(4,128)} %param.12) | copy-start | bytes 49156
  15.3 3.8 %copy-start.7 = (s32[1,1,4]{2,1,0:T(1,128)S(1)}, s32[1,1,4]{2,1,0:T(1,128)}, u32[]{:S(2)}) copy-start(s32[1,1,4]{2,1,0:T(1,128)} %param.10) | copy-start | bytes 52
  15.3 4.1 %copy-start.2 = (s32[1,1,4]{2,1,0:T(1,128)S(1)}, s32[1,1,4]{2,1,0:T(1,128)}, u32[]{:S(2)}) copy-start(s32[1,1,4]{2,1,0:T(1,128)} %param.9) | copy-start | bytes 52
  15.3 4.7 %copy-start.1 = (s32[1,1,4]{2,1,0:T(1,128)S(1)}, s32[1,1,4]{2,1,0:T(1,128)}, u32[]{:S(2)}) copy-start(s32[1,1,4]{2,1,0:T(1,128)} %param.11) | copy-start | bytes 52
  15.3 27.5 %all-to-all-start = ((bf16[4,2,131072]{2,1,0:T(2,128)(2,1)}), bf16[4,2,131072]{2,1,0:T(2,128)(2,1)S(1)}, u32[]{:S(2)}, u32[]{:S(2)}) async-start(bf16[4,2,131072]{2,1,0:T(2,128)(2,1)} %reshape.268), calls=%async_computation | async-start | bytes 4194304 | tf_op jit(solution)/shard_map/all_to_all | solution.py:73
  42.8 58.4 %all-to-all-start.2 = ((s32[8,2,2]{1,2,0:T(2,128)}), s32[8,2,2]{1,2,0:T(2,128)S(1)}, u32[]{:S(2)}, u32[]{:S(2)}) async-start(s32[8,2,2]{1,2,0:T(2,128)} %copy.98), calls=%async_computation.2 | async-start | bytes 16384 | tf_op jit(solution)/shard_map/all_to_all | solution.py:137
  68.4 9.7 %collective-permute-start = (bf16[256,32,2]{0,1,2:T(8,128)(2,1)S(1)}, bf16[256,32,2]{0,1,2:T(8,128)(2,1)S(1)}, u32[]{:S(2)}, u32[]{:S(2)}) collective-permute-start(bf16[256,32,2]{0,1,2:T(8,128)(2,1)S(1)} %copy.90), channel_id=1, source_target_pairs={{0,8},{8,16},{16,24},{1,9},{9,17},{17,25},{2,10},{10,18},{18,26},{... | collective-permute-start | bytes 98312 | tf_op jit(solution)/shard_map/ppermute | solution.py:19
  73.6 8.7 %collective-permute-start.1 = (bf16[256,32,2]{0,1,2:T(8,128)(2,1)S(1)}, bf16[256,32,2]{0,1,2:T(8,128)(2,1)S(1)}, u32[]{:S(2)}, u32[]{:S(2)}) collective-permute-start(bf16[256,32,2]{0,1,2:T(8,128)(2,1)S(1)} %copy.91), channel_id=1, source_target_pairs={{8,0},{16,8},{24,16},{9,1},{17,9},{25,17},{10,2},{18,10},{26,18},{... | collective-permute-start | bytes 98312 | tf_op jit(solution)/shard_map/ppermute | solution.py:22
  86.5 13.6 %copy-start.6 = (s32[1,1,4,1024]{3,2,1,0:T(4,128)S(1)}, s32[1,1,4,1024]{3,2,1,0:T(4,128)}, u32[]{:S(2)}) copy-start(s32[1,1,4,1024]{3,2,1,0:T(4,128)} %param.13) | copy-start | bytes 49156
  90.7 1.9 %copy-start.5 = (bf16[256,32,132]{2,1,0:T(8,128)(2,1)}, bf16[256,32,132]{2,1,0:T(8,128)(2,1)S(1)}, u32[]{:S(2)}) copy-start(bf16[256,32,132]{2,1,0:T(8,128)(2,1)S(1)} %pad_maximum_fusion) | copy-start | bytes 6488068
  93.1 15.8 %collective-permute-start.2 = (bf16[256,2,132]{2,1,0:T(2,128)(2,1)S(1)}, bf16[256,2,132]{2,1,0:T(2,128)(2,1)S(1)}, u32[]{:S(2)}, u32[]{:S(2)}) collective-permute-start(bf16[256,2,132]{2,1,0:T(2,128)(2,1)S(1)} %get-tuple-element.90), channel_id=1, source_target_pairs={{0,1},{1,2},{2,3},{3,4},{4,5},{5,6},{6,7},{8,9},{9,10},{10,11},{11... | collective-permute-start | bytes 405512 | tf_op jit(solution)/shard_map/ppermute | solution.py:19
  97.0 12.1 %collective-permute-start.3 = (bf16[256,2,132]{2,1,0:T(2,128)(2,1)S(1)}, bf16[256,2,132]{2,1,0:T(2,128)(2,1)S(1)}, u32[]{:S(2)}, u32[]{:S(2)}) collective-permute-start(bf16[256,2,132]{2,1,0:T(2,128)(2,1)S(1)} %get-tuple-element.91), channel_id=1, source_target_pairs={{1,0},{2,1},{3,2},{4,3},{5,4},{6,5},{7,6},{9,8},{10,9},{11,10},{12... | collective-permute-start | bytes 405512 | tf_op jit(solution)/shard_map/ppermute | solution.py:22
  116.9 1.7 copy-start.3
  117.0 2.5 %copy-start.4 = (f32[1,36,132]{0,2,1:T(8,128)S(1)}, f32[1,36,132]{0,2,1:T(8,128)}, u32[]{:S(2)}) copy-start(f32[1,36,132]{0,2,1:T(8,128)} %get-tuple-element.135) | copy-start | bytes 57028 | tf_op jit(solution)/shard_map/while
  136.4 1.7 copy-start.3
  136.4 2.5 %copy-start.4 = (f32[1,36,132]{0,2,1:T(8,128)S(1)}, f32[1,36,132]{0,2,1:T(8,128)}, u32[]{:S(2)}) copy-start(f32[1,36,132]{0,2,1:T(8,128)} %get-tuple-element.135) | copy-start | bytes 57028 | tf_op jit(solution)/shard_map/while
  157.5 13.1 %all-to-all-start.3 = ((f32[8,2,128]{2,1,0:T(2,128)}), f32[8,2,128]{2,1,0:T(2,128)S(1)}, u32[]{:S(2)}, u32[]{:S(2)}) async-start(f32[8,2,128]{2,1,0:T(2,128)} %broadcast_select_fusion.1), calls=%async_computation.3 | async-start | bytes 16384 | tf_op jit(solution)/shard_map/all_to_all | solution.py:136
  170.6 12.5 %all-to-all-start.1 = ((f32[8,2,1024]{2,1,0:T(2,128)}), f32[8,2,1024]{2,1,0:T(2,128)S(1)}, u32[]{:S(2)}, u32[]{:S(2)}) async-start(f32[8,2,1024]{2,1,0:T(2,128)} %broadcast_select_fusion), calls=%async_computation.1 | async-start | bytes 131072 | tf_op jit(solution)/shard_map/all_to_all | solution.py:135
where the time goes:
time: 185 us; the launch traced here: 184 us
  local copies, waits for them, and re-layouts  75.2 us (41%)
  other arithmetic  42.9 us (23%)
  starting transfers between devices  33.5 us (18%)
  waiting for transfers between devices  27.1 us (15%)
  loops' own time  4.01 us (2%)
    unnamed x16, local copies, waits for them, and re-layouts  21.3 us
    all_to_all x1, waiting for transfers between devices, per_device(): lax.all_to_all(intensity, 'chan', split_axis=2, concat_axis=0, tiled=True)  20.5 us
    dynamic_update_slice x2, other arithmetic, smooth_tiles(): stacked = lax.map(smooth_block, jnp.arange(chan_blocks, dtype=jnp.int32))  10.8 us
    all_to_all x2, local copies, waits for them, and re-layouts, per_device(): lax.all_to_all(intensity, 'chan', split_axis=2, concat_axis=0, tiled=True)  8.72 us
    add x2, other arithmetic, smooth_block(): sum((weights[offset] * hanning[:, offset:offset + rows_inner, :] for offs...  7.64 us
    concatenate x1, local copies, waits for them, and re-layouts, with_halo(): block = jnp.concatenate([low, block, high], axis=dim)  7.57 us
    slice x3, local copies, waits for them, and re-layouts, with_halo(): lax.slice_in_dim(block, block.shape[dim] - width, None, axis=dim)  6.64 us
    all_to_all x1, starting transfers between devices, per_device(): lax.all_to_all(spectra_slots, 'tile', split_axis=0, concat_axis=0, tiled=...  6.62 us
  transfers between devices with their start and end apart: 8, of which 3 were waited for; matrix products, arithmetic and copies ran while one was open for 31% of the time, Pallas kernels for 0%

commit v1 on v0

--- a/solution.py
+++ b/solution.py
@@ -9,6 +9,32 @@
 CAP = 2
 SRC_DEV = 16
 SIGMA = 1.5
+
+
+def follow_the_screen(block_here, k_dim, unit):
+    newest, v_next = (block_here.shape[:k_dim], block_here.shape[k_dim + 1 :])
+    a_next = block_here.reshape(*newest, unit, -1, *v_next)
+    return jnp.moveaxis(a_next, k_dim, 0)
+
+
+def _enter_indices(obj, dim_i):
+    obj = jnp.moveaxis(obj, 0, dim_i)
+    x_new = obj.shape
+    return obj.reshape(*x_new[:dim_i], x_new[dim_i] * x_new[dim_i + 1], *x_new[dim_i + 2 :])
+
+
+def map_stops_all(work_x, incoming_x, z, device_axis):
+    f_now, last = (lax.axis_size(device_axis), lax.axis_index(device_axis))
+    part_next = follow_the_screen(z, work_x, f_now)
+    idx = 1
+    buffer = [part_next[last]]
+    while idx < f_now:
+        left_arr = part_next[last ^ idx]
+        wide_out = lax.ppermute(left_arr, device_axis, [(i0, i0 ^ idx) for i0 in range(f_now)])
+        buffer.append(wide_out)
+        idx += 1
+    part_next = jnp.stack(buffer)[last ^ jnp.arange(f_now)]
+    return _enter_indices(part_next, incoming_x)
 
 
 def with_halo(block, sides, width):
@@ -70,7 +96,7 @@
 
 
 def per_device(intensity, block_pick, owner_tile, source_index, mask_low, mask_high):
-    regrouped = lax.all_to_all(intensity, "chan", split_axis=2, concat_axis=0, tiled=True)
+    regrouped = map_stops_all(2, incoming_x=0, z=intensity, device_axis="chan")
     framed = with_halo(regrouped, (("chan", 2), ("tile", 1)), RADIUS)
     tile_cube = smooth_tiles(framed)
     chan_total, rows_inner, cols_inner = tile_cube.shape

time: 185 us -> 145 us (0.78)
  local copies, waits for them, and re-layouts: 75.2 us -> 43.7 us
  starting transfers between devices: 33.5 us -> 28.5 us
  waiting for transfers between devices: 27.1 us -> 23.5 us
    all_to_all x1 -> x0, waiting for transfers between devices: 20.5 us -> none  [per_device(): lax.all_to_all(intensity, 'chan', split_axis=2, concat_axis=0, tiled=True)]
    ppermute x0 -> x3, waiting for transfers between devices: none -> 13.4 us  [map_stops_all(): lax.ppermute(left_arr, device_axis, [(i0, i0 ^ idx) for i0 in range(f_now)])]
    unnamed x16 -> x17, local copies, waits for them, and re-layouts: 21.3 us -> 8.33 us
    all_to_all x2 -> x0, local copies, waits for them, and re-layouts: 8.72 us -> none  [per_device(): lax.all_to_all(intensity, 'chan', split_axis=2, concat_axis=0, tiled=True)]
    concatenate x1 -> x0, local copies, waits for them, and re-layouts: 7.57 us -> none  [with_halo(): block = jnp.concatenate([low, block, high], axis=dim)]
    another operation x0 -> x1, local copies, waits for them, and re-layouts: none -> 5.69 us
    reshape x0 -> x2, local copies, waits for them, and re-layouts: none -> 5.28 us  [the longest x1 2.72 us: _enter_indices(): obj.reshape(*x_new[:dim_i], x_new[dim_i] * x_new[dim_i + 1], *x_new[dim_i...]
    ppermute x2 -> x1, local copies, waits for them, and re-layouts: 4.4 us -> 0.04 us  [with_halo(): lax.ppermute(lax.slice_in_dim(block, block.shape[dim] - width, None, axis...]
  transfers between devices with their start and end apart: 8 -> 10, of which waited for: 3 -> 5; matrix products, arithmetic and copies ran while one was open for 31% -> 23% of each run, Pallas kernels for 0% -> 0%
where the time goes in v1:
time: 145 us; the launch traced here: 144 us
  local copies, waits for them, and re-layouts  43.7 us (30%)
  other arithmetic  42.7 us (29%)
  starting transfers between devices  28.5 us (20%)
  waiting for transfers between devices  23.5 us (16%)
  loops' own time  4.01 us (3%)
    ppermute x3, waiting for transfers between devices, map_stops_all(): lax.ppermute(left_arr, device_axis, [(i0, i0 ^ idx) for i0 in range(f_now)])  13.4 us
    dynamic_update_slice x2, other arithmetic, smooth_tiles(): stacked = lax.map(smooth_block, jnp.arange(chan_blocks, dtype=jnp.int32))  10.7 us
    unnamed x17, local copies, waits for them, and re-layouts  8.33 us
    add x2, other arithmetic, smooth_block(): sum((weights[offset] * hanning[:, offset:offset + rows_inner, :] for offs...  7.52 us
    all_to_all x1, waiting for transfers between devices, per_device(): lax.all_to_all(maps_slots, 'tile', split_axis=0, concat_axis=0, tiled=True)  6.16 us
    reduce_sum x2, other arithmetic, per_device(): jnp.sum(masked.reshape(chan_blocks, BCH, block_rows, BPIX, block_cols, BP...  6.11 us
    mul x2, other arithmetic, smooth_block(): after = after * (block_index < chan_blocks - 1).astype(jnp.float32)  6.02 us
    all_to_all x1, starting transfers between devices, per_device(): lax.all_to_all(tags, 'tile', split_axis=0, concat_axis=0, tiled=True)  5.81 us
  transfers between devices with their start and end apart: 10, of which 5 were waited for; matrix products, arithmetic and copies ran while one was open for 23% of the time, Pallas kernels for 0%

profile of v1, /device:TPU:4, one launch (start us, length us, event | category | flops | bytes accessed | tf_op | source)
XLA Modules:
  0.0 143.6 jit_solution(1879163519293932914)
XLA Ops:
  3.2 5.7 %constant_dynamic-slice_fusion.3 = (bf16[64,32,1,128]{3,2,1,0:T(2,128)(2,1)S(1)}, bf16[64,32,1,128]{3,2,1,0:T(2,128)(2,1)S(1)}, bf16[64,32,1,128]{3,2,1,0:T(2,128)(2,1)S(1)}, bf16[64,32,1,128]{3,2,1,0:T(2,128)(2,1)S(1)}) fusion(bf16[64,32,4,128]{3,2,1,0:T(4,128)(2,1)S(1)} %reshape.219, s32[]{:T(128)S(6)} %select_n.108, s32[]{:T(128)S(6)} %select_n.111, ...), kind=kLoop, calls=%fused_computation.85 | loop fusion | bytes 4194320 | tf_op jit(solution)/shard_map/dynamic-slice
  14.6 5.8 %all-to-all-start.1 = ((s32[8,2,2]{1,2,0:T(2,128)}), s32[8,2,2]{1,2,0:T(2,128)S(1)}, u32[]{:S(2)}, u32[]{:S(2)}) async-start(s32[8,2,2]{1,2,0:T(2,128)} %copy.35), calls=%async_computation.1 | async-start | bytes 16384 | tf_op jit(solution)/shard_map/all_to_all | solution.py:163
  21.2 3.0 %collective-permute-done.1 = bf16[64,32,128]{2,1,0:T(8,128)(2,1)} collective-permute-done((bf16[64,32,128]{2,1,0:T(8,128)(2,1)S(1)}, bf16[64,32,128]{2,1,0:T(8,128)(2,1)}, u32[]{:S(2)}, u32[]{:S(2)}) %collective-permute-start.1) | collective-permute-done | bytes 524320 | tf_op jit(solution)/shard_map/ppermute | solution.py:33
  24.1 10.4 %collective-permute-done.2 = bf16[64,32,128]{2,1,0:T(8,128)(2,1)} collective-permute-done((bf16[64,32,128]{2,1,0:T(8,128)(2,1)}, bf16[64,32,128]{2,1,0:T(8,128)(2,1)}, u32[]{:S(2)}, u32[]{:S(2)}) %collective-permute-start.2) | collective-permute-done | bytes 524320 | tf_op jit(solution)/shard_map/ppermute | solution.py:33
  34.6 2.9 %pad_maximum_fusion.1 = bf16[4,64,32,128]{3,2,1,0:T(8,128)(2,1)} fusion(bf16[1,64,32,128]{3,2,1,0:T(8,128)(2,1)} %bitcast.18, bf16[1,64,32,128]{3,2,1,0:T(8,128)(2,1)} %bitcast.17, bf16[1,64,32,128]{3,2,1,0:T(8,128)(2,1)} %bitcast.16, bf16[1,64,32,128]{3,2,1,0:T(8,128)(2,1)S(1)} %bitcast.97), kind=kLoop, calls=%fused_computation.41 | loop fusion | flops 3145728 | bytes 4194304 | tf_op jit(solution)/shard_map/stack | solution.py:36
  40.0 3.0 %fusion.34 = (bf16[256,32,2]{2,1,0:T(8,128)(2,1)}, bf16[256,32,2]{2,1,0:T(8,128)(2,1)}) fusion(bf16[256,32,128]{2,1,0:T(8,128)(2,1)S(1)} %bitcast.94), kind=kLoop, calls=%fused_computation.99 | loop fusion | bytes 131072 | tf_op jit(solution)/shard_map/slice | solution.py:46
  43.0 3.3 %copy.44 = bf16[256,32,2]{0,1,2:T(8,128)(2,1)S(1)} copy(bf16[256,32,2]{2,1,0:T(8,128)(2,1)} %get-tuple-element.92) | data formatting | bytes 65536
  48.4 3.3 %copy.45 = bf16[256,32,2]{0,1,2:T(8,128)(2,1)S(1)} copy(bf16[256,32,2]{2,1,0:T(8,128)(2,1)} %get-tuple-element.93) | data formatting | bytes 65536
  51.7 3.4 %collective-permute-start.4 = (bf16[256,32,2]{0,1,2:T(8,128)(2,1)S(1)}, bf16[256,32,2]{0,1,2:T(8,128)(2,1)S(1)}, u32[]{:S(2)}, u32[]{:S(2)}) collective-permute-start(bf16[256,32,2]{0,1,2:T(8,128)(2,1)S(1)} %copy.45), channel_id=1, source_target_pairs={{8,0},{16,8},{24,16},{9,1},{17,9},{25,17},{10,2},{18,10},{26,18},{... | collective-permute-start | bytes 98312 | tf_op jit(solution)/shard_map/ppermute | solution.py:48
  55.7 2.7 %copy.32 = bf16[256,32,128]{0,2,1:T(8,128)(2,1)} copy(bf16[256,32,128]{2,1,0:T(8,128)(2,1)S(1)} %bitcast.95) | data formatting | bytes 4194304 | tf_op jit(solution)/shard_map/reshape | solution.py:23
  59.6 3.4 %collective-permute-start.5 = (bf16[256,2,132]{0,2,1:T(8,128)(2,1)S(1)}, bf16[256,2,132]{0,2,1:T(8,128)(2,1)S(1)}, u32[]{:S(2)}, u32[]{:S(2)}) collective-permute-start(bf16[256,2,132]{0,2,1:T(8,128)(2,1)S(1)} %get-tuple-element.90), channel_id=1, source_target_pairs={{0,1},{1,2},{2,3},{3,4},{4,5},{5,6},{6,7},{8,9},{9,10},{10,11},{11... | collective-permute-start | bytes 405512 | tf_op jit(solution)/shard_map/ppermute | solution.py:45
  67.3 2.7 %collective-permute-done.6 = bf16[256,2,132]{0,2,1:T(8,128)(2,1)S(1)} collective-permute-done((bf16[256,2,132]{0,2,1:T(8,128)(2,1)S(1)}, bf16[256,2,132]{0,2,1:T(8,128)(2,1)S(1)}, u32[]{:S(2)}, u32[]{:S(2)}) %collective-permute-start.6) | collective-permute-done | bytes 135200 | tf_op jit(solution)/shard_map/ppermute | solution.py:48
  72.3 38.6 %while.12 = (s32[]{:T(128)}, bf16[2,128,32,128]{1,3,2,0:T(8,128)(2,1)}, f32[5]{0:T(128)S(1)}, s32[2]{0:T(128)S(1)}, bf16[256,36,132]{0,2,1:T(8,128)(2,1)S(1)}, /...) while((s32[]{:T(128)}, ...), condition=%wide.region_6.7_spmd, body=%wide.region_5.6_spmd.sunk | while | flops 14994001 | bytes 46544248 | solution.py:94
  74.8 3.0 %convert_multiply_fusion.3 = (f32[1,36,132]{0,2,1:T(8,128)}, f32[1,36,132]{0,2,1:T(8,128)}) fusion(f32[]{:T(128)} %bitcast.85, bf16[256,36,132]{0,2,1:T(8,128)(2,1)S(1)} %get-tuple-element.179, s32[]{:T(128)S(6)} %select_n.147, f32[]{:T(128)} %bitcast.86, s32[]{:T(128)S(6)} %max.7), kind=kLoop, calls=%fused_computation.11.clone.1 | loop fusion | flops 19008 | bytes 57040 | tf_op jit(solution)/shard_map/while/body/eval_jaxpr/mul | solution.py:76
  82.5 3.8 %fusion.43 = f32[128,32,132]{0,2,1:T(8,128)S(1)} fusion(f32[128,36,132]{0,2,1:T(8,128)S(1)} %fusion.41, f32[]{:T(128)} %bitcast.87, f32[]{:T(128)} %bitcast.88, f32[]{:T(128)} %bitcast.89, f32[]{:T(128)} %bitcast.90, f32[]{:T(128)} %bitcast.91), kind=kLoop, calls=%fused_computation.14.clone.1 | loop fusion | flops 4866048 | bytes 12976148 | tf_op jit(solution)/shard_map/while/body/eval_jaxpr/add | solution.py:80
  86.3 5.3 %bitcast_dynamic-update-slice_fusion.2 = bf16[2,128,32,128]{1,3,2,0:T(8,128)(2,1)} fusion(bf16[2,128,32,128]{1,3,2,0:T(8,128)(2,1)} %get-tuple-element.162, s32[]{:T(128)} %get-tuple-element.161, f32[128,32,132]{0,2,1:T(8,128)S(1)} %fusion.43, f32[]{:T(128)} %bitcast.87, f32[]{:T(128)} %bitcast.88, f32[]{:T(128)} %bitcast.89, f32[]{:T(128)} %bitcast.90, ...), kind=kLoop, calls=%fused_computation.33.clone.1 | loop fusion | flops 5242880 | bytes 11537408 | tf_op jit(solution)/shard_map/while/body/jit(dynamic_update_index_in_dim)/dynamic_update_slice | solution.py:94
  94.1 3.0 %convert_multiply_fusion.3 = (f32[1,36,132]{0,2,1:T(8,128)}, f32[1,36,132]{0,2,1:T(8,128)}) fusion(f32[]{:T(128)} %bitcast.85, bf16[256,36,132]{0,2,1:T(8,128)(2,1)S(1)} %get-tuple-element.179, s32[]{:T(128)S(6)} %select_n.147, f32[]{:T(128)} %bitcast.86, s32[]{:T(128)S(6)} %max.7), kind=kLoop, calls=%fused_computation.11.clone.1 | loop fusion | flops 19008 | bytes 57040 | tf_op jit(solution)/shard_map/while/body/eval_jaxpr/mul | solution.py:76
  101.8 3.8 %fusion.43 = f32[128,32,132]{0,2,1:T(8,128)S(1)} fusion(f32[128,36,132]{0,2,1:T(8,128)S(1)} %fusion.41, f32[]{:T(128)} %bitcast.87, f32[]{:T(128)} %bitcast.88, f32[]{:T(128)} %bitcast.89, f32[]{:T(128)} %bitcast.90, f32[]{:T(128)} %bitcast.91), kind=kLoop, calls=%fused_computation.14.clone.1 | loop fusion | flops 4866048 | bytes 12976148 | tf_op jit(solution)/shard_map/while/body/eval_jaxpr/add | solution.py:80
  105.6 5.3 %bitcast_dynamic-update-slice_fusion.2 = bf16[2,128,32,128]{1,3,2,0:T(8,128)(2,1)} fusion(bf16[2,128,32,128]{1,3,2,0:T(8,128)(2,1)} %get-tuple-element.162, s32[]{:T(128)} %get-tuple-element.161, f32[128,32,132]{0,2,1:T(8,128)S(1)} %fusion.43, f32[]{:T(128)} %bitcast.87, f32[]{:T(128)} %bitcast.88, f32[]{:T(128)} %bitcast.89, f32[]{:T(128)} %bitcast.90, ...), kind=kLoop, calls=%fused_computation.33.clone.1 | loop fusion | flops 5242880 | bytes 11537408 | tf_op jit(solution)/shard_map/while/body/jit(dynamic_update_index_in_dim)/dynamic_update_slice | solution.py:94
  110.9 6.1 %fusion.11 = (f32[2,128,128]{1,2,0:T(8,128)S(1)}, f32[2,32,128]{2,1,0:T(8,128)S(1)}) fusion(bf16[2,128,32,128]{1,3,2,0:T(8,128)(2,1)} %get-tuple-element.68, s32[2,32,128]{2,1,0:T(8,128)S(1)} %lt.111, s32[2,32,128]{2,1,0:T(8,128)S(1)} %le.17), kind=kLoop, calls=%fused_computation.35 | loop fusion | flops 7299072 | bytes 2326528 | tf_op jit(solution)/shard_map/reduce_sum | solution.py:144
  119.1 5.7 %all-to-all-start.2 = ((f32[8,2,128]{2,1,0:T(2,128)}), f32[8,2,128]{2,1,0:T(2,128)S(1)}, u32[]{:S(2)}, u32[]{:S(2)}) async-start(f32[8,2,128]{2,1,0:T(2,128)} %broadcast_select_fusion.1), calls=%async_computation.2 | async-start | bytes 16384 | tf_op jit(solution)/shard_map/all_to_all | solution.py:162
  125.6 4.5 %copy.38 = bf16[2,128,32,128]{3,2,1,0:T(8,128)(2,1)} copy(bf16[2,128,32,128]{1,3,2,0:T(8,128)(2,1)} %get-tuple-element.68) | data formatting | bytes 4194304 | tf_op jit(solution)/shard_map/while | solution.py:94
  131.4 4.7 %all-to-all-start = ((f32[8,2,1024]{2,1,0:T(2,128)}), f32[8,2,1024]{2,1,0:T(2,128)S(1)}, u32[]{:S(2)}, u32[]{:S(2)}) async-start(f32[8,2,1024]{2,1,0:T(2,128)} %broadcast_select_fusion), calls=%async_computation | async-start | bytes 131072 | tf_op jit(solution)/shard_map/all_to_all | solution.py:161
  136.9 6.2 %all-to-all-done = f32[8,2,1024]{2,1,0:T(2,128)S(1)} async-done(((f32[8,2,1024]{2,1,0:T(2,128)}), f32[8,2,1024]{2,1,0:T(2,128)S(1)}, u32[]{:S(2)}, u32[]{:S(2)}) %all-to-all-start) | async-done | bytes 65568 | tf_op jit(solution)/shard_map/all_to_all | solution.py:161
  (96 shorter events, 37.7 us)
Async XLA Ops:
  0.6 64.5 %copy-start = (s32[1,1,4,1024]{3,2,1,0:T(4,128)S(1)}, s32[1,1,4,1024]{3,2,1,0:T(4,128)}, u32[]{:S(2)}) copy-start(s32[1,1,4,1024]{3,2,1,0:T(4,128)} %param.12) | copy-start | bytes 49156
  8.9 3.1 %copy-start.6 = (s32[1,1,4]{2,1,0:T(1,128)S(1)}, s32[1,1,4]{2,1,0:T(1,128)}, u32[]{:S(2)}) copy-start(s32[1,1,4]{2,1,0:T(1,128)} %param.10) | copy-start | bytes 52
  8.9 3.5 %copy-start.1 = (s32[1,1,4]{2,1,0:T(1,128)S(1)}, s32[1,1,4]{2,1,0:T(1,128)}, u32[]{:S(2)}) copy-start(s32[1,1,4]{2,1,0:T(1,128)} %param.11) | copy-start | bytes 52
  9.1 4.1 %copy-start.2 = (s32[1,1,4]{2,1,0:T(1,128)S(1)}, s32[1,1,4]{2,1,0:T(1,128)}, u32[]{:S(2)}) copy-start(s32[1,1,4]{2,1,0:T(1,128)} %param.9) | copy-start | bytes 52
  9.1 12.1 %collective-permute-start = (bf16[64,32,128]{2,1,0:T(8,128)(2,1)S(1)}, bf16[64,32,128]{2,1,0:T(8,128)(2,1)}, u32[]{:S(2)}, u32[]{:S(2)}) collective-permute-start(bf16[64,32,128]{2,1,0:T(8,128)(2,1)S(1)} %bitcast.99), channel_id=1, source_target_pairs={{0,8},{8,0},{16,24},{24,16},{1,9},{9,1},{17,25},{25,17},{2,10},{10... | collective-permute-start | bytes 1572872 | tf_op jit(solution)/shard_map/ppermute | solution.py:33
  9.2 14.9 %collective-permute-start.1 = (bf16[64,32,128]{2,1,0:T(8,128)(2,1)S(1)}, bf16[64,32,128]{2,1,0:T(8,128)(2,1)}, u32[]{:S(2)}, u32[]{:S(2)}) collective-permute-start(bf16[64,32,128]{2,1,0:T(8,128)(2,1)S(1)} %bitcast.100), channel_id=1, source_target_pairs={{0,16},{8,24},{16,0},{24,8},{1,17},{9,25},{17,1},{25,9},{2,18},{10... | collective-permute-start | bytes 1572872 | tf_op jit(solution)/shard_map/ppermute | solution.py:33
  10.2 24.4 %collective-permute-start.2 = (bf16[64,32,128]{2,1,0:T(8,128)(2,1)}, bf16[64,32,128]{2,1,0:T(8,128)(2,1)}, u32[]{:S(2)}, u32[]{:S(2)}) collective-permute-start(bf16[64,32,128]{2,1,0:T(8,128)(2,1)} %bitcast.70), channel_id=1, source_target_pairs={{0,24},{8,16},{16,8},{24,0},{1,25},{9,17},{17,9},{25,1},{2,26},{10... | collective-permute-start | bytes 1572872 | tf_op jit(solution)/shard_map/ppermute | solution.py:33
  14.6 52.6 %all-to-all-start.1 = ((s32[8,2,2]{1,2,0:T(2,128)}), s32[8,2,2]{1,2,0:T(2,128)S(1)}, u32[]{:S(2)}, u32[]{:S(2)}) async-start(s32[8,2,2]{1,2,0:T(2,128)} %copy.35), calls=%async_computation.1 | async-start | bytes 16384 | tf_op jit(solution)/shard_map/all_to_all | solution.py:163
  46.3 12.2 %collective-permute-start.3 = (bf16[256,32,2]{0,1,2:T(8,128)(2,1)S(1)}, bf16[256,32,2]{0,1,2:T(8,128)(2,1)S(1)}, u32[]{:S(2)}, u32[]{:S(2)}) collective-permute-start(bf16[256,32,2]{0,1,2:T(8,128)(2,1)S(1)} %copy.44), channel_id=1, source_target_pairs={{0,8},{8,16},{16,24},{1,9},{9,17},{17,25},{2,10},{10,18},{18,26},{... | collective-permute-start | bytes 98312 | tf_op jit(solution)/shard_map/ppermute | solution.py:45
  51.7 6.8 %collective-permute-start.4 = (bf16[256,32,2]{0,1,2:T(8,128)(2,1)S(1)}, bf16[256,32,2]{0,1,2:T(8,128)(2,1)S(1)}, u32[]{:S(2)}, u32[]{:S(2)}) collective-permute-start(bf16[256,32,2]{0,1,2:T(8,128)(2,1)S(1)} %copy.45), channel_id=1, source_target_pairs={{8,0},{16,8},{24,16},{9,1},{17,9},{25,17},{10,2},{18,10},{26,18},{... | collective-permute-start | bytes 98312 | tf_op jit(solution)/shard_map/ppermute | solution.py:48
  58.5 7.6 %copy-start.5 = (s32[1,1,4,1024]{3,2,1,0:T(4,128)S(1)}, s32[1,1,4,1024]{3,2,1,0:T(4,128)}, u32[]{:S(2)}) copy-start(s32[1,1,4,1024]{3,2,1,0:T(4,128)} %param.13) | copy-start | bytes 49156
  59.6 7.7 %collective-permute-start.5 = (bf16[256,2,132]{0,2,1:T(8,128)(2,1)S(1)}, bf16[256,2,132]{0,2,1:T(8,128)(2,1)S(1)}, u32[]{:S(2)}, u32[]{:S(2)}) collective-permute-start(bf16[256,2,132]{0,2,1:T(8,128)(2,1)S(1)} %get-tuple-element.90), channel_id=1, source_target_pairs={{0,1},{1,2},{2,3},{3,4},{4,5},{5,6},{6,7},{8,9},{9,10},{10,11},{11... | collective-permute-start | bytes 405512 | tf_op jit(solution)/shard_map/ppermute | solution.py:45
  63.0 6.9 %collective-permute-start.6 = (bf16[256,2,132]{0,2,1:T(8,128)(2,1)S(1)}, bf16[256,2,132]{0,2,1:T(8,128)(2,1)S(1)}, u32[]{:S(2)}, u32[]{:S(2)}) collective-permute-start(bf16[256,2,132]{0,2,1:T(8,128)(2,1)S(1)} %get-tuple-element.91), channel_id=1, source_target_pairs={{1,0},{2,1},{3,2},{4,3},{5,4},{6,5},{7,6},{9,8},{10,9},{11,10},{12... | collective-permute-start | bytes 405512 | tf_op jit(solution)/shard_map/ppermute | solution.py:48
  78.0 1.7 %copy-start.3 = (f32[1,36,132]{0,2,1:T(8,128)S(1)}, f32[1,36,132]{0,2,1:T(8,128)}, u32[]{:S(2)}) copy-start(f32[1,36,132]{0,2,1:T(8,128)} %get-tuple-element.140) | copy-start | bytes 57028 | tf_op jit(solution)/shard_map/while
  78.0 2.5 %copy-start.4 = (f32[1,36,132]{0,2,1:T(8,128)S(1)}, f32[1,36,132]{0,2,1:T(8,128)}, u32[]{:S(2)}) copy-start(f32[1,36,132]{0,2,1:T(8,128)} %get-tuple-element.139) | copy-start | bytes 57028 | tf_op jit(solution)/shard_map/while
  97.3 1.7 %copy-start.3 = (f32[1,36,132]{0,2,1:T(8,128)S(1)}, f32[1,36,132]{0,2,1:T(8,128)}, u32[]{:S(2)}) copy-start(f32[1,36,132]{0,2,1:T(8,128)} %get-tuple-element.140) | copy-start | bytes 57028 | tf_op jit(solution)/shard_map/while
  97.3 2.5 %copy-start.4 = (f32[1,36,132]{0,2,1:T(8,128)S(1)}, f32[1,36,132]{0,2,1:T(8,128)}, u32[]{:S(2)}) copy-start(f32[1,36,132]{0,2,1:T(8,128)} %get-tuple-element.139) | copy-start | bytes 57028 | tf_op jit(solution)/shard_map/while
  119.1 12.3 %all-to-all-start.2 = ((f32[8,2,128]{2,1,0:T(2,128)}), f32[8,2,128]{2,1,0:T(2,128)S(1)}, u32[]{:S(2)}, u32[]{:S(2)}) async-start(f32[8,2,128]{2,1,0:T(2,128)} %broadcast_select_fusion.1), calls=%async_computation.2 | async-start | bytes 16384 | tf_op jit(solution)/shard_map/all_to_all | solution.py:162
  131.4 11.6 %all-to-all-start = ((f32[8,2,1024]{2,1,0:T(2,128)}), f32[8,2,1024]{2,1,0:T(2,128)S(1)}, u32[]{:S(2)}, u32[]{:S(2)}) async-start(f32[8,2,1024]{2,1,0:T(2,128)} %broadcast_select_fusion), calls=%async_computation | async-start | bytes 131072 | tf_op jit(solution)/shard_map/all_to_all | solution.py:161
